TPU v7x, 32 devices: a whole 2x2x4 slice. The times are simulated.
32 devices in a mesh: grp: 2 (over y), pan: 16 (over z, x, core).
Axes of the slice: x: 2, y: 2, z: 4, core: 2. Of those that a mesh axis runs over, the one named last changes fastest.
Arguments:
- blocks: bfloat16 [1280, 512, 128], P(('grp', 'pan')), parts along dimension 0, may hold values from -6 to 6
- first_block: int32 [1280], P(('grp', 'pan')), parts along dimension 0, may hold values from 0 to 751
- second_block: int32 [1280], P(('grp', 'pan')), parts along dimension 0, may hold values from 0 to 1503
- slot_counts: int32 [32], P(('grp', 'pan')), parts along dimension 0, may hold values from 1 to 40, 240 in all
- ket_first: int32 [8], P('grp'), parts along dimension 0, may hold values from 0 to 751
- ket_second: int32 [8], P('grp'), parts along dimension 0, may hold values from 0 to 1503
- coefficients: bfloat16 [24064, 2000], P(('grp', 'pan')), parts along dimension 0, may hold values from -2 to 2
- mo_index: int32 [128], P('grp'), parts along dimension 0, may hold values from 0 to 1999, as said below
Outputs:
- integrals: float32 [8192, 4096], P(('grp', 'pan')), parts along dimension 0
There are 2 independent parts, one for each index of `grp`. A program takes and returns all parts, laid end to end along the dimension named above; each array names one. Nothing has to cross between parts.
Inputs may be any that keep to these rules, and one draw needn't show every extreme that they name: `slot_counts`: the counts sum to 240; the largest is exactly 40. `mo_index`: distinct orbital numbers.
All inputs are finite; a program needn't handle non-finite values. No bound on the sum of `slot_counts` on one device may be relied on, other than what follows from the above.
Results may differ from a plain program's by a relative error of at most 0.005.
Values may be sent and summed in bfloat16 or wider, within the bound.
No kernel may reach another device: no remote copies, remote signals or barrier semaphores. Data moves between devices by JAX's collectives and lax.ppermute only.
A program may use at most 128 MiB of HBM per device.

v0:
```python
import math

import jax
import jax.numpy as jnp
from jax import lax
from jax.sharding import PartitionSpec as P


def block_rows(chosen, numbers, span_width):
    offsets = jnp.arange(span_width, dtype=jnp.int32)
    row_numbers = numbers[:, None] * span_width + offsets[None, :]
    return jnp.take(chosen, row_numbers, axis=0)


def ket_table(chosen, ket_first, ket_second):
    lambda_rows = block_rows(chosen, ket_first, 16).astype(jnp.float32)
    sigma_rows = block_rows(chosen, ket_second, 8).astype(jnp.float32)
    block_count = lambda_rows.shape[0]
    orbitals = lambda_rows.shape[2]
    product_table = lambda_rows[:, :, None, :, None] * sigma_rows[:, None, :, None, :]
    return product_table.reshape(block_count * 128, orbitals * orbitals).astype(jnp.bfloat16)


def bra_transform(block_data, first_rows, second_rows):
    slot_count = block_data.shape[0]
    ket_width = block_data.shape[1]
    orbitals = first_rows.shape[2]
    group_size = math.gcd(slot_count, max(1, 4096 // ket_width))
    turn_count = slot_count // group_size
    stacked = (
        block_data.reshape(turn_count, group_size, ket_width, 16, 8),
        first_rows.reshape(turn_count, group_size, 16, orbitals),
        second_rows.reshape(turn_count, group_size, 8, orbitals),
    )

    def advance(running, pieces):
        block_part, first_part, second_part = pieces
        halfway = lax.dot_general(
            block_part, first_part, (((2,), (1,)), ((0,), (0,))), preferred_element_type=jnp.float32
        ).astype(jnp.bfloat16)
        product = lax.dot_general(
            halfway, second_part, (((0, 2), (0, 1)), ((), ())), preferred_element_type=jnp.float32
        )
        return (running + product, None)

    running, unused = lax.scan(
        advance, jnp.zeros((ket_width, orbitals, orbitals), jnp.float32), stacked
    )
    return running.reshape(ket_width, orbitals * orbitals)


def shards(
    blocks, first_block, second_block, slot_counts, ket_first, ket_second, coefficients, mo_index
):
    own_rows = jnp.take(coefficients, mo_index, axis=1)
    chosen = lax.all_gather(own_rows, "pan", axis=0, tiled=True)
    product_table = ket_table(chosen, ket_first, ket_second)
    capacity = blocks.shape[0]
    living = (jnp.arange(capacity, dtype=jnp.int32) < slot_counts[0]).astype(jnp.bfloat16)
    first_rows = block_rows(chosen, first_block, 16) * living[:, None, None]
    second_rows = block_rows(chosen, second_block, 8)
    half_done = bra_transform(blocks, first_rows, second_rows)
    own_half = lax.psum_scatter(half_done, "pan", scatter_dimension=1, tiled=True).astype(
        jnp.bfloat16
    )
    return lax.dot_general(
        own_half, product_table, (((0,), (0,)), ((), ())), preferred_element_type=jnp.float32
    )


def solution(mesh):
    placed = (
        P(("grp", "pan"), None, None),
        P(("grp", "pan")),
        P(("grp", "pan")),
        P(("grp", "pan")),
        P("grp"),
        P("grp"),
        P(("grp", "pan"), None),
        P("grp"),
    )
    return jax.shard_map(
        shards, mesh=mesh, in_specs=placed, out_specs=P(("grp", "pan"), None), check_vma=False
    )
```

profile of v0, /device:TPU:0, one launch (start us, length us, event | category | flops | bytes accessed | tf_op | source)
XLA Modules:
  0.0 260.0 jit_solution(13387429850759264746)
XLA Ops:
  12.4 7.9 %copy.23 = bf16[40,512,128]{1,2,0:T(8,128)(2,1)} copy(bf16[40,512,128]{2,1,0:T(8,128)(2,1)} %param.10) | data formatting | bytes 10485760 | tf_op args[0]
  20.5 31.9 %all-gather.3.cloned.1.call-done = bf16[16,752,64]{1,2,0:T(8,128)(2,1)} async-done(((bf16[1,752,64]{1,2,0:T(8,128)(2,1)}), bf16[16,752,64]{1,2,0:T(8,128)(2,1)}) %all-gather.3.cloned.1.call-update) | async-done | bytes 1540112 | tf_op jit(solution)/shard_map/all_gather | solution.py:56
  52.4 4.2 %copy.32 = bf16[16,752,64]{2,1,0:T(8,128)(2,1)} copy(bf16[16,752,64]{1,2,0:T(8,128)(2,1)} %all-gather.3.cloned.1.call-done) | data formatting | bytes 3080192
  56.6 4.0 %gather_fusion.1 = bf16[640,64]{1,0:T(8,128)(2,1)S(1)} fusion(bf16[12032,64]{1,0:T(8,128)(2,1)} %bitcast.53, s32[1024]{0:T(1024)S(1)} %pad_clamp_fusion.3), kind=kCustom, calls=%fused_computation.1 | custom fusion | bytes 166400 | tf_op jit(solution)/shard_map/jit(_take)/gather | solution.py:12
  60.6 3.4 %gather_fusion.2 = bf16[320,64]{1,0:T(8,128)(2,1)S(1)} fusion(bf16[12032,64]{1,0:T(8,128)(2,1)} %bitcast.54, s32[1024]{0:T(1024)S(1)} %pad_clamp_fusion.2), kind=kCustom, calls=%fused_computation.2 | custom fusion | bytes 83200 | tf_op jit(solution)/shard_map/jit(_take)/gather | solution.py:12
  64.3 79.5 %while.11 = (s32[]{:T(128)}, f32[512,64,64]{0,2,1:T(8,128)}, bf16[5,8,512,16,8]{2,4,3,1,0:T(8,128)(2,1)}, bf16[5,8,16,64]{3,2,1,0:T(8,128)(2,1)S(1)}, bf16[5,8,8...) while((s32[]{:T(128)}, f32[512,64,64]{0,2,1:T(8,128)}, bf16[5,8,512,16,8]{2,4,3,1,0:T(8,128)(2,1)}, ...), condition=%wide.region_1.2_spmd.clone, body=%wide.region_0.1_spmd.clone.sunk | while | flops 341835776 | bytes 28360800 | solution.py:46
  64.3 1.3 constant_dynamic-slice_fusion.2
  65.6 3.3 %convolution_convert_fusion.2 = bf16[8,512,8,64]{1,3,2,0:T(8,128)(2,1)} fusion(bf16[1,8,512,16,8]{2,4,3,1,0:T(8,128)(2,1)S(1)} %constant_dynamic-slice_fusion.2, bf16[5,8,16,64]{3,2,1,0:T(8,128)(2,1)S(1)} %get-tuple-element.114, s32[]{:T(128)} %get-tuple-element.104), kind=kOutput, calls=%fused_computation.8.clone.1 | convolution fusion | flops 69206016 | bytes 5275652 | tf_op jit(solution)/shard_map/while/body/eval_jaxpr/dot_general | solution.py:38
  68.9 9.3 %bitcast_add_fusion.2 = f32[512,64,64]{0,2,1:T(8,128)} fusion(f32[512,64,64]{0,2,1:T(8,128)} %get-tuple-element.105, pred[]{:T(512)S(6)} %compare.3, bf16[8,512,8,64]{1,3,2,0:T(8,128)(2,1)} %convolution_convert_fusion.2, bf16[5,8,8,64]{3,2,1,0:T(8,128)(2,1)S(1)} %get-tuple-element.115, s32[]{:T(128)} %get-tuple-element.104), kind=kOutput, calls=%fused_computation.5.clone.1 | convolution fusion | flops 272629760 | bytes 20987908 | tf_op jit(solution)/shard_map/while/body/eval_jaxpr/dot_general | solution.py:41
  78.2 1.3 constant_dynamic-slice_fusion.2
  79.6 3.3 %convolution_convert_fusion.2 = bf16[8,512,8,64]{1,3,2,0:T(8,128)(2,1)} fusion(bf16[1,8,512,16,8]{2,4,3,1,0:T(8,128)(2,1)S(1)} %constant_dynamic-slice_fusion.2, bf16[5,8,16,64]{3,2,1,0:T(8,128)(2,1)S(1)} %get-tuple-element.114, s32[]{:T(128)} %get-tuple-element.104), kind=kOutput, calls=%fused_computation.8.clone.1 | convolution fusion | flops 69206016 | bytes 5275652 | tf_op jit(solution)/shard_map/while/body/eval_jaxpr/dot_general | solution.py:38
  82.9 11.8 %bitcast_add_fusion.2 = f32[512,64,64]{0,2,1:T(8,128)} fusion(f32[512,64,64]{0,2,1:T(8,128)} %get-tuple-element.105, pred[]{:T(512)S(6)} %compare.3, bf16[8,512,8,64]{1,3,2,0:T(8,128)(2,1)} %convolution_convert_fusion.2, bf16[5,8,8,64]{3,2,1,0:T(8,128)(2,1)S(1)} %get-tuple-element.115, s32[]{:T(128)} %get-tuple-element.104), kind=kOutput, calls=%fused_computation.5.clone.1 | convolution fusion | flops 272629760 | bytes 20987908 | tf_op jit(solution)/shard_map/while/body/eval_jaxpr/dot_general | solution.py:41
  96.0 3.3 %convolution_convert_fusion.2 = bf16[8,512,8,64]{1,3,2,0:T(8,128)(2,1)} fusion(bf16[1,8,512,16,8]{2,4,3,1,0:T(8,128)(2,1)S(1)} %constant_dynamic-slice_fusion.2, bf16[5,8,16,64]{3,2,1,0:T(8,128)(2,1)S(1)} %get-tuple-element.114, s32[]{:T(128)} %get-tuple-element.104), kind=kOutput, calls=%fused_computation.8.clone.1 | convolution fusion | flops 69206016 | bytes 5275652 | tf_op jit(solution)/shard_map/while/body/eval_jaxpr/dot_general | solution.py:38
  99.3 11.8 %bitcast_add_fusion.2 = f32[512,64,64]{0,2,1:T(8,128)} fusion(f32[512,64,64]{0,2,1:T(8,128)} %get-tuple-element.105, pred[]{:T(512)S(6)} %compare.3, bf16[8,512,8,64]{1,3,2,0:T(8,128)(2,1)} %convolution_convert_fusion.2, bf16[5,8,8,64]{3,2,1,0:T(8,128)(2,1)S(1)} %get-tuple-element.115, s32[]{:T(128)} %get-tuple-element.104), kind=kOutput, calls=%fused_computation.5.clone.1 | convolution fusion | flops 272629760 | bytes 20987908 | tf_op jit(solution)/shard_map/while/body/eval_jaxpr/dot_general | solution.py:41
  112.4 3.3 %convolution_convert_fusion.2 = bf16[8,512,8,64]{1,3,2,0:T(8,128)(2,1)} fusion(bf16[1,8,512,16,8]{2,4,3,1,0:T(8,128)(2,1)S(1)} %constant_dynamic-slice_fusion.2, bf16[5,8,16,64]{3,2,1,0:T(8,128)(2,1)S(1)} %get-tuple-element.114, s32[]{:T(128)} %get-tuple-element.104), kind=kOutput, calls=%fused_computation.8.clone.1 | convolution fusion | flops 69206016 | bytes 5275652 | tf_op jit(solution)/shard_map/while/body/eval_jaxpr/dot_general | solution.py:38
  115.7 11.7 %bitcast_add_fusion.2 = f32[512,64,64]{0,2,1:T(8,128)} fusion(f32[512,64,64]{0,2,1:T(8,128)} %get-tuple-element.105, pred[]{:T(512)S(6)} %compare.3, bf16[8,512,8,64]{1,3,2,0:T(8,128)(2,1)} %convolution_convert_fusion.2, bf16[5,8,8,64]{3,2,1,0:T(8,128)(2,1)S(1)} %get-tuple-element.115, s32[]{:T(128)} %get-tuple-element.104), kind=kOutput, calls=%fused_computation.5.clone.1 | convolution fusion | flops 272629760 | bytes 20987908 | tf_op jit(solution)/shard_map/while/body/eval_jaxpr/dot_general | solution.py:41
  128.8 3.3 %convolution_convert_fusion.2 = bf16[8,512,8,64]{1,3,2,0:T(8,128)(2,1)} fusion(bf16[1,8,512,16,8]{2,4,3,1,0:T(8,128)(2,1)S(1)} %constant_dynamic-slice_fusion.2, bf16[5,8,16,64]{3,2,1,0:T(8,128)(2,1)S(1)} %get-tuple-element.114, s32[]{:T(128)} %get-tuple-element.104), kind=kOutput, calls=%fused_computation.8.clone.1 | convolution fusion | flops 69206016 | bytes 5275652 | tf_op jit(solution)/shard_map/while/body/eval_jaxpr/dot_general | solution.py:38
  132.1 11.8 %bitcast_add_fusion.2 = f32[512,64,64]{0,2,1:T(8,128)} fusion(f32[512,64,64]{0,2,1:T(8,128)} %get-tuple-element.105, pred[]{:T(512)S(6)} %compare.3, bf16[8,512,8,64]{1,3,2,0:T(8,128)(2,1)} %convolution_convert_fusion.2, bf16[5,8,8,64]{3,2,1,0:T(8,128)(2,1)S(1)} %get-tuple-element.115, s32[]{:T(128)} %get-tuple-element.104), kind=kOutput, calls=%fused_computation.5.clone.1 | convolution fusion | flops 272629760 | bytes 20987908 | tf_op jit(solution)/shard_map/while/body/eval_jaxpr/dot_general | solution.py:41
  145.0 2.9 %gather_fusion.3 = bf16[64,64]{1,0:T(8,128)(2,1)S(1)} fusion(bf16[12032,64]{1,0:T(8,128)(2,1)} %bitcast.55, s32[1024]{0:T(1024)S(1)} %pad_clamp_fusion.1), kind=kCustom, calls=%fused_computation.3 | custom fusion | bytes 16640 | tf_op jit(solution)/shard_map/jit(_take)/gather | solution.py:12
  147.8 2.9 %gather_fusion.4 = bf16[32,64]{1,0:T(8,128)(2,1)S(1)} fusion(bf16[12032,64]{1,0:T(8,128)(2,1)} %bitcast.56, s32[1024]{0:T(1024)S(1)} %pad_clamp_fusion), kind=kCustom, calls=%fused_computation.4 | custom fusion | bytes 8320 | tf_op jit(solution)/shard_map/jit(_take)/gather | solution.py:12
  150.9 6.1 %multiply_convert_fusion = bf16[4,16,8,64,64]{4,3,2,1,0:T(8,128)(2,1)} fusion(f32[4,8,64]{2,1,0:T(8,128)S(1)} %fusion.18, f32[4,16,64]{2,1,0:T(8,128)S(1)} %select_convert_fusion), kind=kLoop, calls=%fused_computation.17 | loop fusion | flops 4194304 | bytes 4218880 | tf_op jit(solution)/shard_map/convert_element_type | solution.py:21
  157.1 12.3 %convert_element_type.38 = bf16[512,4096]{1,0:T(8,128)(2,1)} reshape(bf16[4,16,8,64,64]{4,3,2,1,0:T(8,128)(2,1)} %multiply_convert_fusion) | data formatting | bytes 8388608 | tf_op jit(solution)/shard_map/convert_element_type | solution.py:21
  169.4 78.1 %reduce-scatter.2.cloned.1.call-done = f32[512,256]{0,1:T(8,128)} async-done(((f32[512,4096]{0,1:T(8,128)}), f32[512,256]{0,1:T(8,128)}) %reduce-scatter.2.cloned.1.call-update) | async-done | bytes 524304 | tf_op jit(solution)/shard_map/reduce_scatter | solution.py:63
  247.5 5.6 %fusion.10 = f32[256,4096]{1,0:T(8,128)} fusion(bf16[512,4096]{1,0:T(8,128)(2,1)} %convert_element_type.38, f32[512,256]{0,1:T(8,128)} %reduce-scatter.2.cloned.1.call-done), kind=kOutput, calls=%fused_computation.18 | convolution fusion | flops 1073872896 | bytes 8912896 | tf_op jit(solution)/shard_map/dot_general | solution.py:66
  (46 shorter events, 10.9 us)
Async XLA Ops:
  6.5 1.9 copy-start
  6.5 45.9 %all-gather.3.cloned.1.call-start = ((), (), s32[]{:S(2)}) async-start(), calls=%async_computation.2 | async-start | bytes 1671168 | tf_op jit(solution)/shard_map/all_gather | solution.py:56
  9.9 237.6 %reduce-scatter.2.cloned.1.call-start = ((), (), s32[]{:S(2)}) async-start(), calls=%async_computation.1 | async-start | bytes 8912896 | tf_op jit(solution)/shard_map/reduce_scatter | solution.py:63
  143.8 0.7 copy-start.1
  143.8 0.8 copy-start.2
Sparse Core Ops, SparseCore 0:
  10.0 42.3 all-gather.2
  144.0 103.4 reduce-scatter.1
where the time goes:
time: 261 us; the launch traced here: 260 us
  waiting for transfers between devices  110 us (42%)
  matrix products  78.5 us (30%)
  local copies, waits for them, and re-layouts  46.3 us (18%)
  between operations  14.2 us (5%)
  other arithmetic  10.9 us (4%)
    reduce_scatter x1, waiting for transfers between devices, shards(): lax.psum_scatter(half_done, 'pan', scatter_dimension=1, tiled=True)  78.1 us
    dot_general x5, matrix products, advance(): lax.dot_general(halfway, second_part, (((0, 2), (0, 1)), ((), ())), prefe...  56.3 us
    all_gather x1, waiting for transfers between devices, shards(): chosen = lax.all_gather(own_rows, 'pan', axis=0, tiled=True)  31.9 us
    dot_general x5, matrix products, advance(): lax.dot_general(block_part, first_part, (((2,), (1,)), ((0,), (0,))), pre...  16.6 us
    gather x4, local copies, waits for them, and re-layouts, block_rows(): return jnp.take(chosen, row_numbers, axis=0)  13.1 us
    unnamed x8, local copies, waits for them, and re-layouts  13 us
    convert_element_type x1, local copies, waits for them, and re-layouts, ket_table(): product_table.reshape(block_count * 128, orbitals * orbitals)  12.3 us
    dynamic_slice x5, local copies, waits for them, and re-layouts, bra_transform(): lax.scan(advance, jnp.zeros((ket_width, orbitals, orbitals), jnp.float32)...  6.63 us
  transfers between devices with their start and end apart: 2, of which 2 were waited for; matrix products, arithmetic and copies ran while one was open for 13% of the time, Pallas kernels for 0%

commit v1 on v0

v1 whole, which is shorter than its diff:
```python
import functools

import jax
import jax.numpy as jnp
from jax import lax
from jax.experimental import pallas as pl
from jax.experimental.pallas import tpu as pltpu
from jax.sharding import PartitionSpec as P

GROUP = 32
LANES = 128
UNIT = 16384
BF = jnp.bfloat16
F32 = jnp.float32


def spread(kind):
    row = lax.broadcasted_iota(jnp.int32, (LANES, LANES), 0)
    col = lax.broadcasted_iota(jnp.int32, (LANES, LANES), 1)
    source = col // 8 if kind == "a" else col % 8
    return (row == source).astype(F32).astype(BF)


def table_piece(table, code, target):
    unit = code // UNIT
    lane = code % UNIT
    start = pl.multiple_of((lane // LANES) * LANES, LANES)
    piece = table[unit, :, pl.ds(start, LANES)].astype(F32)
    shift = lax.rem(target - lane % LANES + 2 * LANES, LANES)
    return pltpu.roll(piece, shift, 1)


def load_table(parts, table, sems):
    copies = []
    at = 0
    for n, part in enumerate(parts):
        units = part.shape[0]
        copies.append(pltpu.make_async_copy(part, table.at[pl.ds(at, units)], sems.at[n]))
        at += units
    return copies


def bra_kernel(part_count, chunk, fcode, scode, info, *refs):
    parts, refs = refs[:part_count], refs[part_count:]
    own, other = refs[:2]
    out_count = len(refs) - 2 - 8
    outs = refs[2 : 2 + out_count]
    table, blk, wide, half, second, total, table_sems, block_sems = refs[2 + out_count :]
    orbitals = table.shape[1]
    capacity = own.shape[0]
    kh = blk.shape[1]
    width = chunk * out_count
    own_live, other_live = info[0], info[1]
    k_start = pl.multiple_of(info[2], 128)
    live = own_live + other_live

    copies = load_table(parts, table, table_sems)
    for copy in copies:
        copy.start()

    def own_copy(n):
        return pltpu.make_async_copy(
            own.at[n, pl.ds(k_start, kh)], blk.at[n], block_sems.at[n // GROUP]
        )

    def other_copy(n):
        return pltpu.make_async_copy(
            other.at[n - own_live], blk.at[n], block_sems.at[n // GROUP]
        )

    def start_own(n, carry):
        own_copy(n).start()
        return carry

    def start_other(n, carry):
        other_copy(n).start()
        return carry

    lax.fori_loop(0, own_live, start_own, 0)
    lax.fori_loop(own_live, live, start_other, 0)
    total[...] = jnp.zeros_like(total)
    half[...] = jnp.zeros_like(half)
    lanes = lax.broadcasted_iota(jnp.int32, (8, LANES), 1)
    diagonal = (lanes % 8 == lax.broadcasted_iota(jnp.int32, (8, LANES), 0)).astype(F32)
    spread_a = spread("a")
    for copy in copies:
        copy.wait()

    def do_group(g, carry):
        base = g * GROUP
        count = jnp.minimum(live - base, GROUP)

        def wait_one(n, carry):
            pltpu.make_async_copy(
                own.at[0, pl.ds(0, kh)], blk.at[n], block_sems.at[g]
            ).wait()
            return carry

        lax.fori_loop(base, base + count, wait_one, 0)
        second[...] = jnp.zeros_like(second)

        def do_pair(p, carry):
            results = []
            for u in range(2):
                place = 2 * p + u
                n = jnp.minimum(base + place, live - 1)
                slot = jnp.where(n < own_live, n, capacity + n - own_live)
                piece = table_piece(table, fcode[slot], 0)
                wide[u] = jnp.dot(piece.astype(BF), spread_a, preferred_element_type=F32)
                rows = []
                for q in range(out_count):
                    start = pl.multiple_of(info[3 + q], 8)
                    for r in range(chunk):
                        row = wide[u, pl.ds(start + r, 1), :]
                        rows.append(jnp.broadcast_to(row, (8, LANES)) * diagonal)
                factor = jnp.concatenate(rows, axis=0).astype(BF)
                result = lax.dot_general(
                    factor, blk[n], (((1,), (1,)), ((), ())), preferred_element_type=F32
                )
                results.append(result.reshape(width, 8, kh))
                piece = table_piece(table, scode[slot], 8 * lax.rem(place, 16))
                side = place // 16
                low = 8 * lax.rem(place, 16)
                wanted = lax.broadcasted_iota(jnp.int32, (orbitals, LANES), 1)
                keep = (wanted >= low) & (wanted < low + 8) & (base + place < live)
                second[side] = jnp.where(keep, piece, second[side])
            both = jnp.concatenate(results, axis=1).astype(BF)
            half[:, pl.ds(pl.multiple_of(p * 16, 16), 16), :] = both
            return carry

        lax.fori_loop(0, (count + 1) // 2, do_pair, 0)
        weights = jnp.concatenate([second[0], second[1]], axis=1).astype(BF)
        for i in range(width):
            rows = pl.ds(i * orbitals, orbitals)
            total[rows, :] += jnp.dot(weights, half[i], preferred_element_type=F32)
        return carry

    lax.fori_loop(0, (live + GROUP - 1) // GROUP, do_group, 0)
    size = chunk * orbitals
    for q in range(out_count):
        outs[q][...] = total[q * size : (q + 1) * size, :].astype(outs[q].dtype)


def bra_transform(parts, own, other, fcode, scode, info, chunk, out_count, out_type):
    orbitals = parts[0].shape[1]
    capacity, kp, pair = own.shape
    kh = other.shape[1]
    units = sum(part.shape[0] for part in parts)
    groups = -(-2 * capacity // GROUP)
    rows = chunk * orbitals
    anywhere = pl.BlockSpec(memory_space=pl.ANY)
    width = chunk * out_count
    return pl.pallas_call(
        functools.partial(bra_kernel, len(parts), chunk),
        out_shape=[jax.ShapeDtypeStruct((rows, kh), out_type)] * out_count,
        grid_spec=pltpu.PrefetchScalarGridSpec(
            num_scalar_prefetch=3,
            grid=(),
            in_specs=[anywhere] * (len(parts) + 2),
            out_specs=[pl.BlockSpec(memory_space=pltpu.VMEM)] * out_count,
            scratch_shapes=[
                pltpu.VMEM((units, orbitals, parts[0].shape[2]), BF),
                pltpu.VMEM((2 * capacity, kh, pair), BF),
                pltpu.VMEM((2, orbitals, LANES), F32),
                pltpu.VMEM((width, 8 * GROUP, kh), BF),
                pltpu.VMEM((2, orbitals, LANES), F32),
                pltpu.VMEM((rows * out_count, kh), F32),
                pltpu.SemaphoreType.DMA((len(parts),)),
                pltpu.SemaphoreType.DMA((groups,)),
            ],
        ),
        compiler_params=pltpu.CompilerParams(vmem_limit_bytes=40 * 2**20),
        cost_estimate=pl.CostEstimate(
            flops=2 * 2 * capacity * 8 * width * pair * kh, bytes_accessed=8 * 2**20, transcendentals=0
        ),
        name="bra_transform",
    )(fcode, scode, info, *parts, own, other)


def ket_kernel(part_count, code1, code2, *refs):
    parts = refs[:part_count]
    out, table, first, sems = refs[part_count:]
    orbitals = table.shape[1]
    copies = load_table(parts, table, sems)
    for copy in copies:
        copy.start()
    for copy in copies:
        copy.wait()
    for kb in range(out.shape[1] // LANES):
        piece = table_piece(table, code1[kb], 0)
        first[...] = jnp.dot(piece.astype(BF), spread("a"), preferred_element_type=F32)
        piece = table_piece(table, code2[kb], 0)
        last = jnp.dot(piece.astype(BF), spread("b"), preferred_element_type=F32)
        for r in range(orbitals):
            row = jnp.broadcast_to(first[r : r + 1, :], (orbitals, LANES))
            rows = pl.ds(r * orbitals, orbitals)
            out[rows, kb * LANES : (kb + 1) * LANES] = (row * last).astype(BF)


def ket_table(parts, code1, code2):
    orbitals = parts[0].shape[1]
    units = sum(part.shape[0] for part in parts)
    shape = (orbitals * orbitals, code1.shape[0] * LANES)
    return pl.pallas_call(
        functools.partial(ket_kernel, len(parts)),
        out_shape=jax.ShapeDtypeStruct(shape, BF),
        grid_spec=pltpu.PrefetchScalarGridSpec(
            num_scalar_prefetch=2,
            grid=(),
            in_specs=[pl.BlockSpec(memory_space=pl.ANY)] * len(parts),
            out_specs=pl.BlockSpec(memory_space=pltpu.VMEM),
            scratch_shapes=[
                pltpu.VMEM((units, orbitals, parts[0].shape[2]), BF),
                pltpu.VMEM((orbitals, LANES), F32),
                pltpu.SemaphoreType.DMA((len(parts),)),
            ],
        ),
        compiler_params=pltpu.CompilerParams(vmem_limit_bytes=24 * 2**20),
        cost_estimate=pl.CostEstimate(
            flops=2 * 2**20, bytes_accessed=6 * 2**20, transcendentals=0
        ),
        name="ket_table",
    )(code1, code2, *parts)


def permute(array, mask, count):
    return lax.ppermute(array, "pan", [(i, i ^ mask) for i in range(count)])


def added(*arrays):
    result = arrays[0].astype(F32)
    for array in arrays[1:]:
        result = result + array.astype(F32)
    return result.astype(BF)


def shards(
    count, blocks, first_block, second_block, slot_counts, ket_first, ket_second, coefficients, mo_index
):
    me = lax.axis_index("pan").astype(jnp.int32)
    core = me % 2
    capacity, kp, pair = blocks.shape
    kh = kp // 2
    own_ao, nmo = coefficients.shape
    swap = functools.partial(permute, mask=1, count=count)

    picks = (mo_index[:, None] == jnp.arange(nmo, dtype=jnp.int32)[None, :]).astype(BF)
    mine = lax.dot_general(
        picks, coefficients, (((1,), (1,)), ((), ())), preferred_element_type=F32
    ).astype(BF)
    orbitals = mine.shape[0]

    leaving = lax.dynamic_slice_in_dim(blocks, (1 - core) * kh, kh, axis=1)
    other = swap(leaving)
    numbers = jnp.concatenate([first_block, second_block, slot_counts])
    other_numbers = swap(numbers)
    firsts = jnp.concatenate([first_block, other_numbers[:capacity]]) * 16
    seconds = jnp.concatenate([second_block, other_numbers[capacity : 2 * capacity]]) * 8
    lives = [slot_counts[0], other_numbers[2 * capacity]]

    small = count == 16 and own_ao % 16 == 0
    if small:
        mine = jnp.pad(mine, ((0, 0), (0, -own_ao % LANES)))
        along_z = [None, None, None, None]
        for s in (3, 2, 1):
            along_z[s] = permute(mine, 4 * s, count)
        along_z[0] = mine
        near = jnp.stack(along_z)
        far = permute(near, 2, count)
        parts = [near, swap(near), far, swap(far)]

        def encode(rows):
            away = (rows // own_ao) ^ me
            unit = ((away >> 1) & 1) * 8 + (away & 1) * 4 + (away >> 2)
            return unit * UNIT + rows % own_ao
    else:
        parts = [lax.all_gather(mine, "pan", axis=1, tiled=True)[None]]

        def encode(rows):
            return rows

    fcode, scode = encode(firsts), encode(seconds)
    ahead = jnp.arange(ket_first.shape[0], dtype=jnp.int32)
    turned = (ahead + core * (ket_first.shape[0] // 2)) % ket_first.shape[0]
    table = ket_table(
        parts,
        encode(jnp.take(ket_first, turned) * 16),
        encode(jnp.take(ket_second, turned) * 8),
    )

    if small:
        my_z, my_x = me // 4, (me // 2) % 2
        order = (3, 2, 1, 0)
        chunk = orbitals // 8
        results = []
        for x in (1 - my_x, my_x):
            starts = [((my_z ^ s) * 2 + x) * chunk for s in order]
            info = jnp.stack([*lives, core * kh, *starts]).astype(jnp.int32)
            results.append(
                bra_transform(parts, blocks, other, fcode, scode, info, chunk, 4, BF)
            )
        arrived = [permute(piece, 2, count) for piece in results[0]]
        kept = results[1]
        three = permute(added(kept[0], arrived[0]), 4, count)
        two = permute(added(kept[1], arrived[1], three), 8, count)
        one = permute(added(kept[2], arrived[2]), 4, count)
        done = added(kept[3], arrived[3], one, two)
    else:
        info = jnp.stack([*lives, core * kh, jnp.int32(0)]).astype(jnp.int32)
        (partial,) = bra_transform(parts, blocks, other, fcode, scode, info, orbitals, 1, F32)
        sides = [list(range(c, count, 2)) for c in range(2)]
        done = lax.psum_scatter(
            partial, "pan", scatter_dimension=0, tiled=True, axis_index_groups=sides
        ).astype(BF)
    rows = done.shape[0] // 2
    keep = lax.dynamic_slice_in_dim(done, core * rows, rows, axis=0)
    give = lax.dynamic_slice_in_dim(done, (1 - core) * rows, rows, axis=0)
    half_rounded = jnp.concatenate([keep, swap(give)], axis=1)
    return lax.dot_general(
        half_rounded, table, (((1,), (1,)), ((), ())), preferred_element_type=F32
    )


def solution(mesh):
    placed = (
        P(("grp", "pan"), None, None),
        P(("grp", "pan")),
        P(("grp", "pan")),
        P(("grp", "pan")),
        P("grp"),
        P("grp"),
        P(("grp", "pan"), None),
        P("grp"),
    )
    return jax.shard_map(
        functools.partial(shards, mesh.shape["pan"]),
        mesh=mesh,
        in_specs=placed,
        out_specs=P(("grp", "pan"), None),
        check_vma=False,
    )
```

time: 261 us -> 114 us (0.44)
  the two profiles are of different devices: /device:TPU:0 before, /device:TPU:3 now
where the time goes in v1:
time: 114 us; the launch traced here: 115 us
  starting transfers between devices  51.9 us (46%)
  waiting for transfers between devices  22.1 us (19%)
  Pallas kernels  17.8 us (16%)
  local copies, waits for them, and re-layouts  14.3 us (13%)
  other arithmetic  4.2 us (4%)
  matrix products  3.99 us (4%)
    ppermute x16, starting transfers between devices, permute(): return lax.ppermute(array, 'pan', [(i, i ^ mask) for i in range(count)])  51.9 us
    ppermute x16, waiting for transfers between devices, permute(): return lax.ppermute(array, 'pan', [(i, i ^ mask) for i in range(count)])  22.1 us
    pallas_call x2, Pallas kernels, bra_transform(): pl.pallas_call(functools.partial(bra_kernel, len(parts), chunk), out_shap...  14.7 us
    unnamed x22, local copies, waits for them, and re-layouts  7.09 us
    convert_element_type x4, other arithmetic, added(): return result.astype(BF)  3.92 us
    dynamic_slice x1, local copies, waits for them, and re-layouts, shards(): leaving = lax.dynamic_slice_in_dim(blocks, (1 - core) * kh, kh, axis=1)  3.7 us
    dot_general x1, matrix products, shards(): lax.dot_general(half_rounded, table, (((1,), (1,)), ((), ())), preferred_...  3.3 us
    pallas_call x1, Pallas kernels, ket_table(): pl.pallas_call(functools.partial(ket_kernel, len(parts)), out_shape=jax.S...  3.09 us
  transfers between devices with their start and end apart: 16, of which 7 were waited for; matrix products, arithmetic and copies ran while one was open for 6% of the time, Pallas kernels for 9%

profile of v1, /device:TPU:3, one launch (start us, length us, event | category | flops | bytes accessed | tf_op | source)
XLA Modules:
  0.0 115.1 jit_solution(18302283154785463493)
XLA Ops:
  0.0 3.7 %constant_dynamic-slice_fusion.2 = bf16[40,256,128]{2,1,0:T(8,128)(2,1)} fusion(bf16[40,512,128]{2,1,0:T(8,128)(2,1)} %refs_4_.3, s32[]{:T(128)S(6)} %select_n.79), kind=kLoop, calls=%fused_computation.30 | loop fusion | bytes 5242884 | tf_op jit(solution)/shard_map/dynamic_slice | solution.py:253
  5.1 2.4 %collective-permute-start.2 = (bf16[64,768]{1,0:T(8,128)(2,1)S(1)}, bf16[64,768]{1,0:T(8,128)(2,1)S(1)}, u32[]{:S(2)}, u32[]{:S(2)}) collective-permute-start(bf16[64,768]{1,0:T(8,128)(2,1)S(1)} %get-tuple-element.25), channel_id=1, source_target_pairs={{0,8},{1,9},{2,10},{3,11},{4,12},{5,13},{6,14},{7,15},{8,0},{9,1},... | collective-permute-start | bytes 294920 | tf_op jit(solution)/shard_map/ppermute | solution.py:227
  7.5 1.3 %collective-permute-start.1 = (bf16[64,768]{1,0:T(8,128)(2,1)S(1)}, bf16[64,768]{1,0:T(8,128)(2,1)S(1)}, u32[]{:S(2)}, u32[]{:S(2)}) collective-permute-start(bf16[64,768]{1,0:T(8,128)(2,1)S(1)} %get-tuple-element.25), channel_id=1, source_target_pairs={{0,4},{1,5},{2,6},{3,7},{4,0},{5,1},{6,2},{7,3},{8,12},{9,13},{10,... | collective-permute-start | bytes 294920 | tf_op jit(solution)/shard_map/ppermute | solution.py:227
  8.8 3.8 %collective-permute-done.2 = bf16[64,768]{1,0:T(8,128)(2,1)S(1)} collective-permute-done((bf16[64,768]{1,0:T(8,128)(2,1)S(1)}, bf16[64,768]{1,0:T(8,128)(2,1)S(1)}, u32[]{:S(2)}, u32[]{:S(2)}) %collective-permute-start.2) | collective-permute-done | bytes 98336 | tf_op jit(solution)/shard_map/ppermute | solution.py:227
  12.6 3.2 %collective-permute-done.3 = bf16[64,768]{1,0:T(8,128)(2,1)S(1)} collective-permute-done((bf16[64,768]{1,0:T(8,128)(2,1)S(1)}, bf16[64,768]{1,0:T(8,128)(2,1)S(1)}, u32[]{:S(2)}, u32[]{:S(2)}) %collective-permute-start.3) | collective-permute-done | bytes 98336 | tf_op jit(solution)/shard_map/ppermute | solution.py:227
  16.8 1.2 %collective-permute-start.4 = (bf16[4,64,768]{2,1,0:T(8,128)(2,1)S(1)}, bf16[4,64,768]{2,1,0:T(8,128)(2,1)}, u32[]{:S(2)}, u32[]{:S(2)}) collective-permute-start(bf16[4,64,768]{2,1,0:T(8,128)(2,1)S(1)} %pad_maximum_fusion.refs_0_), channel_id=1, source_target_pairs={{0,1},{1,0},{2,3},{3,2},{4,5},{5,4},{6,7},{7,6},{8,9},{9,8},{10,11... | collective-permute-start | bytes 1179656 | tf_op jit(solution)/shard_map/ppermute | solution.py:227
  18.0 7.8 %collective-permute-done.5.refs_2_ = bf16[4,64,768]{2,1,0:T(8,128)(2,1)} collective-permute-done((bf16[4,64,768]{2,1,0:T(8,128)(2,1)S(1)}, bf16[4,64,768]{2,1,0:T(8,128)(2,1)}, u32[]{:S(2)}, u32[]{:S(2)}) %collective-permute-start.5) | collective-permute-done | bytes 393248 | tf_op jit(solution)/shard_map/ppermute | solution.py:227
  25.8 1.7 %collective-permute-start.6 = (bf16[4,64,768]{2,1,0:T(8,128)(2,1)}, bf16[4,64,768]{2,1,0:T(8,128)(2,1)}, u32[]{:S(2)}, u32[]{:S(2)}) collective-permute-start(bf16[4,64,768]{2,1,0:T(8,128)(2,1)} %collective-permute-done.5.refs_2_), channel_id=1, source_target_pairs={{0,1},{1,0},{2,3},{3,2},{4,5},{5,4},{6,7},{7,6},{8,9},{9,8},{10,11... | collective-permute-start | bytes 1179656 | tf_op jit(solution)/shard_map/ppermute | solution.py:227
  27.7 1.2 %collective-permute-done = s32[81]{0:T(128)S(1)} collective-permute-done((s32[81]{0:T(128)S(1)}, s32[81]{0:T(128)S(1)}, u32[]{:S(2)}, u32[]{:S(2)}) %collective-permute-start) | collective-permute-done | bytes 356 | tf_op jit(solution)/shard_map/ppermute | solution.py:227
  30.5 2.5 %copy-done.1 = bf16[40,512,128]{2,1,0:T(8,128)(2,1)S(1)} copy-done((bf16[40,512,128]{2,1,0:T(8,128)(2,1)S(1)}, bf16[40,512,128]{2,1,0:T(8,128)(2,1)}, u32[]{:S(2)}) %copy-start.1) | copy-done | bytes 5242904
  33.0 7.7 %bra_transform.3 = (bf16[512,256]{1,0:T(8,128)(2,1)}, bf16[512,256]{1,0:T(8,128)(2,1)S(1)}, bf16[512,256]{1,0:T(8,128)(2,1)S(1)}, bf16[512,256]{1,0:T(8,128)(2,1)}) custom-call(s32[80]{0:T(128)S(1)} %get-tuple-element.28.fcode, s32[80]{0:T(128)S(1)} %get-tuple-element.29.scode, s32[7]{0:T(128)S(1)} %stack.64.info, ...), custom_call_target="tpu_custom_call" | custom-call | flops 1342177280 | bytes 8388608 | tf_op jit(solution)/shard_map/bra_transform/pallas_call | solution.py:153
  42.9 1.5 %collective-permute-start.9 = (bf16[512,256]{1,0:T(8,128)(2,1)}, bf16[512,256]{1,0:T(8,128)(2,1)S(1)}, u32[]{:S(2)}, u32[]{:S(2)}) collective-permute-start(bf16[512,256]{1,0:T(8,128)(2,1)} %copy-done.5), channel_id=1, source_target_pairs={{0,2},{1,3},{2,0},{3,1},{4,6},{5,7},{6,4},{7,5},{8,10},{9,11},{10,... | collective-permute-start | bytes 786440 | tf_op jit(solution)/shard_map/ppermute | solution.py:227
  44.5 2.5 %copy-done.2 = bf16[40,512,128]{2,1,0:T(8,128)(2,1)S(1)} copy-done((bf16[40,512,128]{2,1,0:T(8,128)(2,1)S(1)}, bf16[40,512,128]{2,1,0:T(8,128)(2,1)}, u32[]{:S(2)}) %copy-start.2) | copy-done | bytes 5242904
  47.0 7.0 %bra_transform.2 = (bf16[512,256]{1,0:T(8,128)(2,1)S(1)}, bf16[512,256]{1,0:T(8,128)(2,1)S(1)}, bf16[512,256]{1,0:T(8,128)(2,1)S(1)}, bf16[512,256]{1,0:T(8,128)(2,1)S(1)}) custom-call(s32[80]{0:T(128)S(1)} %get-tuple-element.28.fcode, s32[80]{0:T(128)S(1)} %get-tuple-element.29.scode, s32[7]{0:T(128)S(1)} %stack.54.info, ...), custom_call_target="tpu_custom_call" | custom-call | flops 1342177280 | bytes 8388608 | tf_op jit(solution)/shard_map/bra_transform/pallas_call | solution.py:153
  54.7 1.0 add_convert_fusion.2
  55.8 1.1 collective-permute-start.8
  57.7 1.4 %collective-permute-start.10 = (bf16[512,256]{1,0:T(8,128)(2,1)}, bf16[512,256]{1,0:T(8,128)(2,1)}, u32[]{:S(2)}, u32[]{:S(2)}) collective-permute-start(bf16[512,256]{1,0:T(8,128)(2,1)} %add_convert_fusion.3), channel_id=1, source_target_pairs={{0,4},{1,5},{2,6},{3,7},{4,0},{5,1},{6,2},{7,3},{8,12},{9,13},{10,... | collective-permute-start | bytes 786440 | tf_op jit(solution)/shard_map/ppermute | solution.py:227
  59.1 2.3 %collective-permute-done.11 = bf16[512,256]{1,0:T(8,128)(2,1)S(1)} collective-permute-done((bf16[512,256]{1,0:T(8,128)(2,1)}, bf16[512,256]{1,0:T(8,128)(2,1)S(1)}, u32[]{:S(2)}, u32[]{:S(2)}) %collective-permute-start.11) | collective-permute-done | bytes 262176 | tf_op jit(solution)/shard_map/ppermute | solution.py:227
  63.2 28.8 %collective-permute-start.14 = (bf16[512,256]{1,0:T(8,128)(2,1)}, bf16[512,256]{1,0:T(8,128)(2,1)}, u32[]{:S(2)}, u32[]{:S(2)}) collective-permute-start(bf16[512,256]{1,0:T(8,128)(2,1)} %add_convert_fusion.1), channel_id=1, source_target_pairs={{0,8},{1,9},{2,10},{3,11},{4,12},{5,13},{6,14},{7,15},{8,0},{9,1},... | collective-permute-start | bytes 786440 | tf_op jit(solution)/shard_map/ppermute | solution.py:227
  93.3 2.8 %collective-permute-done.14 = bf16[512,256]{1,0:T(8,128)(2,1)} collective-permute-done((bf16[512,256]{1,0:T(8,128)(2,1)}, bf16[512,256]{1,0:T(8,128)(2,1)}, u32[]{:S(2)}, u32[]{:S(2)}) %collective-permute-start.14) | collective-permute-done | bytes 262176 | tf_op jit(solution)/shard_map/ppermute | solution.py:227
  96.0 1.3 %add_convert_fusion = bf16[512,256]{1,0:T(8,128)(2,1)S(1)} fusion(bf16[512,256]{1,0:T(8,128)(2,1)} %collective-permute-done.14, bf16[512,256]{1,0:T(8,128)(2,1)} %collective-permute-done.10, bf16[512,256]{1,0:T(8,128)(2,1)} %collective-permute-done.8, bf16[512,256]{1,0:T(8,128)(2,1)} %copy-done.3), kind=kLoop, calls=%fused_computation.3 | loop fusion | flops 1048576 | bytes 1310720 | tf_op jit(solution)/shard_map/convert_element_type | solution.py:234
  97.4 11.3 %collective-permute-start.15 = (bf16[256,256]{1,0:T(8,128)(2,1)S(1)}, bf16[256,256]{1,0:T(8,128)(2,1)S(1)}, u32[]{:S(2)}, u32[]{:S(2)}) collective-permute-start(bf16[256,256]{1,0:T(8,128)(2,1)S(1)} %get-tuple-element.23), channel_id=1, source_target_pairs={{0,1},{1,0},{2,3},{3,2},{4,5},{5,4},{6,7},{7,6},{8,9},{9,8},{10,11... | collective-permute-start | bytes 393224 | tf_op jit(solution)/shard_map/ppermute | solution.py:227
  108.7 3.1 %ket_table.1 = bf16[4096,512]{1,0:T(8,128)(2,1)S(1)} custom-call(s32[4]{0:T(128)S(1)} %get-tuple-element.30.code1, s32[4]{0:T(128)S(1)} %get-tuple-element.31.code2, bf16[4,64,768]{2,1,0:T(8,128)(2,1)S(1)} %pad_maximum_fusion.refs_0_, bf16[4,64,768]{2,1,0:T(8,128)(2,1)} %collective-permute-done.4.refs_1_, ...), custom_call_target="tpu_custom_call" | custom-call | flops 2097152 | bytes 6291456 | tf_op jit(solution)/shard_map/ket_table/pallas_call | solution.py:204
  111.8 3.3 %fusion = f32[256,4096]{1,0:T(8,128)} fusion(bf16[4096,512]{1,0:T(8,128)(2,1)S(1)} %ket_table.1, bf16[256,256]{1,0:T(8,128)(2,1)S(1)} %collective-permute-done.15, bf16[256,256]{1,0:T(8,128)(2,1)S(1)} %get-tuple-element.22), kind=kOutput, calls=%fused_computation.9 | convolution fusion | flops 1074266112 | bytes 8650752 | tf_op jit(solution)/shard_map/dot_general | solution.py:319
  (54 shorter events, 10.4 us)
Async XLA Ops:
  0.0 4.4 %copy-start = (bf16[752,2000]{0,1:T(8,128)(2,1)S(1)}, bf16[752,2000]{0,1:T(8,128)(2,1)}, u32[]{:S(2)}) copy-start(bf16[752,2000]{0,1:T(8,128)(2,1)} %param.16) | copy-start | bytes 9024004
  0.0 4.4 %copy-start.10 = (s32[64]{0:T(128)S(1)}, s32[64]{0:T(128)}, u32[]{:S(2)}) copy-start(s32[64]{0:T(128)} %param.17) | copy-start | bytes 772
  0.0 27.6 %copy-start.8 = (s32[40]{0:T(128)S(1)}, s32[40]{0:T(128)}, u32[]{:S(2)}) copy-start(s32[40]{0:T(128)} %param.12) | copy-start | bytes 484
  0.0 27.6 %copy-start.9 = (s32[40]{0:T(128)S(1)}, s32[40]{0:T(128)}, u32[]{:S(2)}) copy-start(s32[40]{0:T(128)} %param.11) | copy-start | bytes 484
  3.7 26.8 %collective-permute-start.7 = (bf16[40,256,128]{2,1,0:T(8,128)(2,1)}, bf16[40,256,128]{2,1,0:T(8,128)(2,1)}, u32[]{:S(2)}, u32[]{:S(2)}) collective-permute-start(bf16[40,256,128]{2,1,0:T(8,128)(2,1)} %constant_dynamic-slice_fusion.2), channel_id=1, source_target_pairs={{0,1},{1,0},{2,3},{3,2},{4,5},{5,4},{6,7},{7,6},{8,9},{9,8},{10,11... | collective-permute-start | bytes 7864328 | tf_op jit(solution)/shard_map/ppermute | solution.py:227
  5.1 7.5 %collective-permute-start.2 = (bf16[64,768]{1,0:T(8,128)(2,1)S(1)}, bf16[64,768]{1,0:T(8,128)(2,1)S(1)}, u32[]{:S(2)}, u32[]{:S(2)}) collective-permute-start(bf16[64,768]{1,0:T(8,128)(2,1)S(1)} %get-tuple-element.25), channel_id=1, source_target_pairs={{0,8},{1,9},{2,10},{3,11},{4,12},{5,13},{6,14},{7,15},{8,0},{9,1},... | collective-permute-start | bytes 294920 | tf_op jit(solution)/shard_map/ppermute | solution.py:227
  7.5 5.1 %collective-permute-start.1 = (bf16[64,768]{1,0:T(8,128)(2,1)S(1)}, bf16[64,768]{1,0:T(8,128)(2,1)S(1)}, u32[]{:S(2)}, u32[]{:S(2)}) collective-permute-start(bf16[64,768]{1,0:T(8,128)(2,1)S(1)} %get-tuple-element.25), channel_id=1, source_target_pairs={{0,4},{1,5},{2,6},{3,7},{4,0},{5,1},{6,2},{7,3},{8,12},{9,13},{10,... | collective-permute-start | bytes 294920 | tf_op jit(solution)/shard_map/ppermute | solution.py:227
  8.8 7.0 %collective-permute-start.3 = (bf16[64,768]{1,0:T(8,128)(2,1)S(1)}, bf16[64,768]{1,0:T(8,128)(2,1)S(1)}, u32[]{:S(2)}, u32[]{:S(2)}) collective-permute-start(bf16[64,768]{1,0:T(8,128)(2,1)S(1)} %get-tuple-element.25), channel_id=1, source_target_pairs={{0,12},{1,13},{2,14},{3,15},{4,8},{5,9},{6,10},{7,11},{8,4},{9,5},... | collective-permute-start | bytes 294920 | tf_op jit(solution)/shard_map/ppermute | solution.py:227
  15.9 10.0 %collective-permute-start.5 = (bf16[4,64,768]{2,1,0:T(8,128)(2,1)S(1)}, bf16[4,64,768]{2,1,0:T(8,128)(2,1)}, u32[]{:S(2)}, u32[]{:S(2)}) collective-permute-start(bf16[4,64,768]{2,1,0:T(8,128)(2,1)S(1)} %pad_maximum_fusion.refs_0_), channel_id=1, source_target_pairs={{0,2},{1,3},{2,0},{3,1},{4,6},{5,7},{6,4},{7,5},{8,10},{9,11},{10,... | collective-permute-start | bytes 1179656 | tf_op jit(solution)/shard_map/ppermute | solution.py:227
  16.8 13.7 %collective-permute-start.4 = (bf16[4,64,768]{2,1,0:T(8,128)(2,1)S(1)}, bf16[4,64,768]{2,1,0:T(8,128)(2,1)}, u32[]{:S(2)}, u32[]{:S(2)}) collective-permute-start(bf16[4,64,768]{2,1,0:T(8,128)(2,1)S(1)} %pad_maximum_fusion.refs_0_), channel_id=1, source_target_pairs={{0,1},{1,0},{2,3},{3,2},{4,5},{5,4},{6,7},{7,6},{8,9},{9,8},{10,11... | collective-permute-start | bytes 1179656 | tf_op jit(solution)/shard_map/ppermute | solution.py:227
  25.8 4.7 %collective-permute-start.6 = (bf16[4,64,768]{2,1,0:T(8,128)(2,1)}, bf16[4,64,768]{2,1,0:T(8,128)(2,1)}, u32[]{:S(2)}, u32[]{:S(2)}) collective-permute-start(bf16[4,64,768]{2,1,0:T(8,128)(2,1)} %collective-permute-done.5.refs_2_), channel_id=1, source_target_pairs={{0,1},{1,0},{2,3},{3,2},{4,5},{5,4},{6,7},{7,6},{8,9},{9,8},{10,11... | collective-permute-start | bytes 1179656 | tf_op jit(solution)/shard_map/ppermute | solution.py:227
  27.7 1.3 %collective-permute-start = (s32[81]{0:T(128)S(1)}, s32[81]{0:T(128)S(1)}, u32[]{:S(2)}, u32[]{:S(2)}) collective-permute-start(s32[81]{0:T(128)S(1)} %pad_add_fusion), channel_id=1, source_target_pairs={{0,1},{1,0},{2,3},{3,2},{4,5},{5,4},{6,7},{7,6},{8,9},{9,8},{10,11... | collective-permute-start | bytes 980 | tf_op jit(solution)/shard_map/ppermute | solution.py:227
  30.5 2.5 %copy-start.1 = (bf16[40,512,128]{2,1,0:T(8,128)(2,1)S(1)}, bf16[40,512,128]{2,1,0:T(8,128)(2,1)}, u32[]{:S(2)}) copy-start(bf16[40,512,128]{2,1,0:T(8,128)(2,1)} %refs_4_.3) | copy-start | bytes 15728644
  42.2 12.5 %collective-permute-start.12 = (bf16[512,256]{1,0:T(8,128)(2,1)}, bf16[512,256]{1,0:T(8,128)(2,1)}, u32[]{:S(2)}, u32[]{:S(2)}) collective-permute-start(bf16[512,256]{1,0:T(8,128)(2,1)} %get-tuple-element.21), channel_id=1, source_target_pairs={{0,2},{1,3},{2,0},{3,1},{4,6},{5,7},{6,4},{7,5},{8,10},{9,11},{10,... | collective-permute-start | bytes 786440 | tf_op jit(solution)/shard_map/ppermute | solution.py:227
  42.9 14.0 %collective-permute-start.9 = (bf16[512,256]{1,0:T(8,128)(2,1)}, bf16[512,256]{1,0:T(8,128)(2,1)S(1)}, u32[]{:S(2)}, u32[]{:S(2)}) collective-permute-start(bf16[512,256]{1,0:T(8,128)(2,1)} %copy-done.5), channel_id=1, source_target_pairs={{0,2},{1,3},{2,0},{3,1},{4,6},{5,7},{6,4},{7,5},{8,10},{9,11},{10,... | collective-permute-start | bytes 786440 | tf_op jit(solution)/shard_map/ppermute | solution.py:227
  44.4 17.0 %collective-permute-start.11 = (bf16[512,256]{1,0:T(8,128)(2,1)}, bf16[512,256]{1,0:T(8,128)(2,1)S(1)}, u32[]{:S(2)}, u32[]{:S(2)}) collective-permute-start(bf16[512,256]{1,0:T(8,128)(2,1)} %copy-done.4), channel_id=1, source_target_pairs={{0,2},{1,3},{2,0},{3,1},{4,6},{5,7},{6,4},{7,5},{8,10},{9,11},{10,... | collective-permute-start | bytes 786440 | tf_op jit(solution)/shard_map/ppermute | solution.py:227
  44.5 2.5 %copy-start.2 = (bf16[40,512,128]{2,1,0:T(8,128)(2,1)S(1)}, bf16[40,512,128]{2,1,0:T(8,128)(2,1)}, u32[]{:S(2)}) copy-start(bf16[40,512,128]{2,1,0:T(8,128)(2,1)} %refs_4_.3) | copy-start | bytes 15728644
  47.0 45.0 %copy-start.6 = (s32[4]{0:T(128)S(1)}, s32[4]{0:T(128)}, u32[]{:S(2)}) copy-start(s32[4]{0:T(128)} %param.15) | copy-start | bytes 52
  47.0 45.7 %copy-start.7 = (s32[4]{0:T(128)S(1)}, s32[4]{0:T(128)}, u32[]{:S(2)}) copy-start(s32[4]{0:T(128)} %param.14) | copy-start | bytes 52
  55.7 6.7 %collective-permute-start.13 = (bf16[512,256]{1,0:T(8,128)(2,1)S(1)}, bf16[512,256]{1,0:T(8,128)(2,1)S(1)}, u32[]{:S(2)}, u32[]{:S(2)}) collective-permute-start(bf16[512,256]{1,0:T(8,128)(2,1)S(1)} %add_convert_fusion.2), channel_id=1, source_target_pairs={{0,4},{1,5},{2,6},{3,7},{4,0},{5,1},{6,2},{7,3},{8,12},{9,13},{10,... | collective-permute-start | bytes 786440 | tf_op jit(solution)/shard_map/ppermute | solution.py:227
  55.8 37.5 %collective-permute-start.8 = (bf16[512,256]{1,0:T(8,128)(2,1)}, bf16[512,256]{1,0:T(8,128)(2,1)}, u32[]{:S(2)}, u32[]{:S(2)}) collective-permute-start(bf16[512,256]{1,0:T(8,128)(2,1)} %get-tuple-element.15), channel_id=1, source_target_pairs={{0,2},{1,3},{2,0},{3,1},{4,6},{5,7},{6,4},{7,5},{8,10},{9,11},{10,... | collective-permute-start | bytes 786440 | tf_op jit(solution)/shard_map/ppermute | solution.py:227
  57.7 35.6 %collective-permute-start.10 = (bf16[512,256]{1,0:T(8,128)(2,1)}, bf16[512,256]{1,0:T(8,128)(2,1)}, u32[]{:S(2)}, u32[]{:S(2)}) collective-permute-start(bf16[512,256]{1,0:T(8,128)(2,1)} %add_convert_fusion.3), channel_id=1, source_target_pairs={{0,4},{1,5},{2,6},{3,7},{4,0},{5,1},{6,2},{7,3},{8,12},{9,13},{10,... | collective-permute-start | bytes 786440 | tf_op jit(solution)/shard_map/ppermute | solution.py:227
  63.2 32.8 %collective-permute-start.14 = (bf16[512,256]{1,0:T(8,128)(2,1)}, bf16[512,256]{1,0:T(8,128)(2,1)}, u32[]{:S(2)}, u32[]{:S(2)}) collective-permute-start(bf16[512,256]{1,0:T(8,128)(2,1)} %add_convert_fusion.1), channel_id=1, source_target_pairs={{0,8},{1,9},{2,10},{3,11},{4,12},{5,13},{6,14},{7,15},{8,0},{9,1},... | collective-permute-start | bytes 786440 | tf_op jit(solution)/shard_map/ppermute | solution.py:227
  97.4 14.4 %collective-permute-start.15 = (bf16[256,256]{1,0:T(8,128)(2,1)S(1)}, bf16[256,256]{1,0:T(8,128)(2,1)S(1)}, u32[]{:S(2)}, u32[]{:S(2)}) collective-permute-start(bf16[256,256]{1,0:T(8,128)(2,1)S(1)} %get-tuple-element.23), channel_id=1, source_target_pairs={{0,1},{1,0},{2,3},{3,2},{4,5},{5,4},{6,7},{7,6},{8,9},{9,8},{10,11... | collective-permute-start | bytes 393224 | tf_op jit(solution)/shard_map/ppermute | solution.py:227
  (3 other events, 2.1 us)
